TPU v7x, 128 devices: a whole 4x4x4 slice. The times are simulated.
128 devices in a mesh: row: 16 (over z_lo, x, core), col: 8 (over y, z_hi).
Axes of the slice: x: 4, y: 4, z: 4 (z_hi: 2, z_lo: 2; z = z_hi * 2 + z_lo), core: 2. Of those that a mesh axis runs over, the one named last changes fastest.
Arguments:
- matrix: bfloat16 [9216, 9216], P('row', 'col'), may hold values from -8 to 8
- inverse_factor: bfloat16 [9216, 9216], P('row', 'col'), may hold values from -2 to 2, as said below
Outputs:
- reduced: float32 [9216, 9216], P('col', 'row')
Inputs may be any that keep to these rules, and one draw needn't show every extreme that they name: inverse_factor is zero above its diagonal; its diagonal lies in 0.4 to 1.6.
All inputs are finite; a program needn't handle non-finite values.
Results may differ from a plain program's by a relative error of at most 0.0029.
Values may be sent and summed in bfloat16 or wider, within the bound.
A program may use at most 128 MiB of HBM per device.

v0:
```python
import jax
import jax.numpy as jnp
from jax import lax
from jax.sharding import PartitionSpec as P


def body(matrix, inverse_factor):
    lower_rows = lax.all_gather(inverse_factor, "col", axis=1, tiled=True)
    left = jnp.dot(
        lower_rows,
        lax.all_gather(matrix, "row", axis=0, tiled=True),
        preferred_element_type=jnp.float32,
    ).astype(jnp.bfloat16)
    contract = (((1,), (1,)), ((), ()))
    column_panel = lax.all_gather(left, "row", axis=0, tiled=True)
    return lax.psum_scatter(
        lax.dot_general(column_panel, inverse_factor, contract, preferred_element_type=jnp.float32),
        "col",
        scatter_dimension=0,
        tiled=True,
    )


def solution(mesh):
    in_specs = (P("row", "col"), P("row", "col"))
    out_specs = P("col", "row")
    return jax.shard_map(body, mesh=mesh, in_specs=in_specs, out_specs=out_specs, check_vma=False)
```

profile of v0, /device:TPU:63, one launch (start us, length us, event | category | flops | bytes accessed | tf_op | source)
XLA Modules:
  0.0 642.0 jit_solution(5476868637387477038)
XLA Ops:
  6.5 0.0 all-gather.4.cloned.1.call-start
  6.5 0.7 all-gather.4.cloned.1.call-update
  7.3 0.0 all-gather.6.cloned.1.call-start
  7.3 0.7 all-gather.6.cloned.1.call-update
  8.0 0.0 copy-start
  8.0 0.0 all-gather.8.cloned.1.call-start
  8.1 129.2 %all-gather.4.cloned.1.call-done = bf16[576,9216]{1,0:T(8,128)(2,1)} async-done(((bf16[576,1152]{1,0:T(8,128)(2,1)}), bf16[576,9216]{1,0:T(8,128)(2,1)}) %all-gather.4.cloned.1.call-update) | async-done | bytes 10616848 | tf_op jit(solution)/shard_map/all_gather | solution.py:8
  137.2 114.8 %all-gather.6.cloned.1.call-done = bf16[9216,1152]{1,0:T(8,128)(2,1)} async-done(((bf16[576,1152]{1,0:T(8,128)(2,1)}), bf16[9216,1152]{1,0:T(8,128)(2,1)}) %all-gather.6.cloned.1.call-update) | async-done | bytes 21233680 | tf_op jit(solution)/shard_map/all_gather | solution.py:11
  252.0 19.5 %convolution_convert_fusion = bf16[576,1152]{1,0:T(8,128)(2,1)} fusion(bf16[576,9216]{1,0:T(8,128)(2,1)} %all-gather.4.cloned.1.call-done, bf16[9216,1152]{1,0:T(8,128)(2,1)} %all-gather.6.cloned.1.call-done), kind=kOutput, calls=%fused_computation | convolution fusion | flops 12231254016 | bytes 33177600 | tf_op jit(solution)/shard_map/dot_general | solution.py:9
  271.5 0.0 all-gather.8.cloned.1.call-update
  271.5 0.0 reduce-scatter.2.cloned.1.call-start
  271.6 113.4 %all-gather.8.cloned.1.call-done = bf16[9216,1152]{1,0:T(8,128)(2,1)} async-done(((bf16[576,1152]{1,0:T(8,128)(2,1)}), bf16[9216,1152]{1,0:T(8,128)(2,1)}) %all-gather.8.cloned.1.call-update) | async-done | bytes 21233680 | tf_op jit(solution)/shard_map/all_gather | solution.py:15
  385.0 0.0 copy-done
  385.0 22.1 %fusion = f32[9216,576]{0,1:T(8,128)} fusion(bf16[9216,1152]{1,0:T(8,128)(2,1)} %all-gather.8.cloned.1.call-done, bf16[576,1152]{1,0:T(8,128)(2,1)S(1)} %copy-done), kind=kOutput, calls=%fused_computation.1 | convolution fusion | flops 12230590464 | bytes 43794432 | tf_op jit(solution)/shard_map/dot_general | solution.py:17
  407.1 0.0 reduce-scatter.2.cloned.1.call-update
  407.1 228.4 %reduce-scatter.2.cloned.1.call-done = f32[1152,576]{0,1:T(8,128)} async-done(((f32[9216,576]{0,1:T(8,128)}), f32[1152,576]{0,1:T(8,128)}) %reduce-scatter.2.cloned.1.call-update) | async-done | bytes 2654224 | tf_op jit(solution)/shard_map/reduce_scatter | solution.py:16
Async XLA Ops:
  6.5 130.7 %all-gather.4.cloned.1.call-start = ((), (), s32[]{:S(2)}) async-start(), calls=%async_computation.1 | async-start | bytes 11943936 | tf_op jit(solution)/shard_map/all_gather | solution.py:8
  7.3 244.7 %all-gather.6.cloned.1.call-start = ((), (), s32[]{:S(2)}) async-start(), calls=%async_computation.2 | async-start | bytes 22560768 | tf_op jit(solution)/shard_map/all_gather | solution.py:11
  8.0 377.0 %copy-start = (bf16[576,1152]{1,0:T(8,128)(2,1)S(1)}, bf16[576,1152]{1,0:T(8,128)(2,1)}, u32[]{:S(2)}) copy-start(bf16[576,1152]{1,0:T(8,128)(2,1)} %param.3) | copy-start | bytes 3981316
  8.0 377.0 %all-gather.8.cloned.1.call-start = ((), (), s32[]{:S(2)}) async-start(), calls=%async_computation.3 | async-start | bytes 22560768 | tf_op jit(solution)/shard_map/all_gather | solution.py:15
  271.5 364.0 %reduce-scatter.2.cloned.1.call-start = ((), (), s32[]{:S(2)}) async-start(), calls=%async_computation.4 | async-start | bytes 23887872 | tf_op jit(solution)/shard_map/reduce_scatter | solution.py:16
Sparse Core Ops, SparseCore 0:
  9.7 127.4 all-gather.3
  138.9 113.0 all-gather.5
  271.6 113.3 all-gather.7
  407.2 228.2 reduce-scatter.1
where the time goes:
time: 646 us; the launch traced here: 642 us
  waiting for transfers between devices  587 us (91%)
  matrix products  41.5 us (6%)
  between operations  13.1 us (2%)
    reduce_scatter x1, waiting for transfers between devices, body(): lax.psum_scatter(lax.dot_general(column_panel, inverse_factor, contract,...  228 us
    all_gather x1, waiting for transfers between devices, body(): lower_rows = lax.all_gather(inverse_factor, 'col', axis=1, tiled=True)  129 us
    all_gather x1, waiting for transfers between devices, body(): lax.all_gather(matrix, 'row', axis=0, tiled=True)  115 us
    all_gather x1, waiting for transfers between devices, body(): column_panel = lax.all_gather(left, 'row', axis=0, tiled=True)  113 us
    dot_general x1, matrix products, body(): lax.dot_general(column_panel, inverse_factor, contract, preferred_element...  22.1 us
    dot_general x1, matrix products, body(): jnp.dot(lower_rows, lax.all_gather(matrix, 'row', axis=0, tiled=True), pr...  19.5 us
  transfers between devices with their start and end apart: 4, of which 4 were waited for; matrix products, arithmetic and copies ran while one was open for 0% of the time, Pallas kernels for 0%

commit v1 on v0

v1 whole, which is shorter than its diff:
```python
import jax
import jax.numpy as jnp
from jax import lax
from jax.experimental import pallas as pl
from jax.experimental.pallas import tpu as pltpu
from jax.sharding import PartitionSpec as P

BF16, F32 = jnp.bfloat16, jnp.float32


def kernel(a_ref, l_ref, o_ref, abuf, lbuf, fbuf, acc, lbf, ssem, rsem, csem):
    rows, cols = a_ref.shape
    half = rows // 2
    row, c = lax.axis_index("row"), lax.axis_index("col")
    h, p = row % 2, row // 2
    x, zl = p % 4, p // 4
    y, zh = c // 2, c % 2

    def chip(px, pz):
        return (pz % 2) * 4 + px % 4

    def on_row(pp):
        return (pp * 2 + h, c)

    xp, xm = on_row(chip(x + 1, zl)), on_row(chip(x + 3, zl))
    zp = on_row(chip(x, zl + 1))
    sib = (p * 2 + 1 - h, c)
    yp = (row, ((y + 1) % 4) * 2 + zh)
    ym = (row, ((y + 3) % 4) * 2 + zh)
    hp = (row, y * 2 + 1 - zh)

    t_chip = chip(x + y + 2 * h, zh)
    t_dst = (t_chip * 2 + h, p)

    def kap(px, pz, hh):
        return 2 * ((px - c % 4 - 2 * hh + 8) % 4) + pz % 2

    t_src = (c * 2 + h, kap(x, zl, h))
    t_self = (p == c) & (t_chip == p)

    send_n = [0]
    recv_ids = {}
    sends = []

    def rid(role):
        return recv_ids.setdefault(role, len(recv_ids))

    def send(src, dst, role, device):
        i = send_n[0]
        send_n[0] += 1
        cp = pltpu.make_async_remote_copy(
            src, dst, ssem.at[i], rsem.at[rid(role)], device_id=device,
            device_id_type=pl.DeviceIdType.MESH)
        cp.start()
        sends.append(cp)

    def wait(ref, role):
        pltpu.make_async_remote_copy(
            ref, ref, ssem.at[0], rsem.at[rid(role)], device_id=xp,
            device_id_type=pl.DeviceIdType.MESH).wait_recv()

    barrier = pltpu.get_barrier_semaphore()
    for device in (xp, xm, zp, sib, yp, ym, hp):
        pl.semaphore_signal(barrier, inc=1, device_id=device, device_id_type=pl.DeviceIdType.MESH)

    @pl.when(jnp.logical_not(t_self))
    def _():
        for device in (t_dst, t_src):
            pl.semaphore_signal(barrier, inc=1, device_id=device, device_id_type=pl.DeviceIdType.MESH)

    pl.semaphore_wait(barrier, jnp.where(t_self, 7, 9))

    def a_at(d, q, hh, lo=0, n=rows):
        start = pl.multiple_of((chip(x + d, zl + q) * 2 + hh) * rows + lo, 16)
        return abuf.at[pl.ds(start, n)]

    def l_at(d, q, lo=0, n=rows):
        return lbuf.at[((y + d) % 4) * 2 + (zh + q) % 2, pl.ds(lo, n)]

    def a_send(src, d, q, lo, n, role, device):
        send(src, a_at(d, q, h, lo, n), role, device)

    own_a = a_at(0, 0, h)
    own_l = l_at(0, 0)
    send(a_ref, own_a, "a30", xp)
    send(l_ref, own_l, "l30", yp)
    send(a_ref, own_a, "a10", xm)
    send(l_ref, own_l, "l10", ym)
    send(a_ref, own_a, "a01", zp)
    send(l_ref, own_l, "l01", hp)
    send(a_ref, own_a, "sa00", sib)
    ca = pltpu.make_async_copy(a_ref, own_a, csem.at[0])
    cl = pltpu.make_async_copy(l_ref, own_l, csem.at[1])
    ca.start()
    cl.start()
    acc[...] = jnp.zeros_like(acc)
    o_ref[...] = jnp.zeros_like(o_ref)

    def got(d, q, part=""):
        lo, n = {"": (0, rows), "t": (0, half), "b": (half, half)}[part]
        return a_at(d, q, h, lo, n), l_at(d, q, lo, n), a_at(d, q, 1 - h, lo, n)

    def arrive(d, q, part=""):
        tag = f"{d}{q}{part}"
        ra, rl, _ = got(d, q, part)
        wait(ra, "a" + tag)
        wait(rl, "l" + tag)
        send(ra, ra, "sa" + tag, sib)

    def forward(d, q, part, role, which):
        ra, rl, _ = got(d, q, part)
        send(ra, ra, "a" + role, xp if which else xm)
        send(rl, rl, "l" + role, yp if which else ym)

    def from_sib(d, q, part=""):
        wait(got(d, q, part)[2], f"sa{d}{q}{part}")

    def stage_of(d, q):
        near = jnp.where(d == 0, 1, jnp.where(d == 2, 2, 1))
        far = jnp.where(d == 0, 1, jnp.where(d == 2, 4, 3))
        return jnp.where(q == 0, near, far)

    tile = 384

    def left_stage(stage):
        def step(k, carry):
            sa = stage_of((k % 4 - x + 4) % 4, (k // 4 + zl) % 2)
            sl = stage_of((k // 2 - y + 4) % 4, (k % 2 + zh) % 2)

            @pl.when((jnp.maximum(sa, sl) == stage) & (k <= p))
            def _():
                krow = pl.multiple_of(k * cols, cols)

                def part(j, carry):
                    at = pl.ds(pl.multiple_of(j * tile, tile), tile)
                    acc[:, at] += jnp.dot(
                        lbuf[k], abuf[pl.ds(krow, cols), at], preferred_element_type=F32)
                    return carry

                lax.fori_loop(0, cols // tile, part, 0)
            return carry

        lax.fori_loop(0, 8, step, 0)

    arrive(3, 0)
    forward(3, 0, "t", "20t", True)
    arrive(1, 0)
    forward(1, 0, "b", "20b", False)
    arrive(0, 1)
    forward(0, 1, "", "31", True)
    forward(0, 1, "", "11", False)
    ca.wait()
    cl.wait()
    from_sib(0, 0)
    from_sib(3, 0)
    from_sib(1, 0)
    from_sib(0, 1)
    left_stage(1)
    arrive(2, 0, "t")
    arrive(2, 0, "b")
    from_sib(2, 0, "t")
    from_sib(2, 0, "b")
    left_stage(2)
    arrive(3, 1)
    forward(3, 1, "t", "21t", True)
    arrive(1, 1)
    forward(1, 1, "b", "21b", False)
    from_sib(3, 1)
    from_sib(1, 1)
    left_stage(3)
    arrive(2, 1, "t")
    arrive(2, 1, "b")
    from_sib(2, 1, "t")
    from_sib(2, 1, "b")
    left_stage(4)

    parts = ((0, "t"), (half, "b"))
    lbf[...] = acc[...].astype(BF16)

    def f_at(d, q, hh, lo):
        start = pl.multiple_of(hh * rows + lo, 16)
        return fbuf.at[kap(x + d, zl + q, hh), pl.ds(start, half)]

    turn = []
    for lo, tag in parts:
        src = lbf.at[pl.ds(lo, half)]
        dst = fbuf.at[c, pl.ds(pl.multiple_of(h * rows + lo, 16), half)]
        i = send_n[0]
        send_n[0] += 1
        rsem_at = rsem.at[rid("f00" + tag)]
        cp = pltpu.make_async_remote_copy(
            src, dst, ssem.at[i], rsem_at, device_id=t_dst,
            device_id_type=pl.DeviceIdType.MESH)
        turn.append(cp)

        @pl.when(jnp.logical_not(t_self))
        def _():
            cp.start()

        @pl.when(t_self)
        def _():
            pltpu.make_async_copy(src, dst, rsem_at).start()

    def f_send(d, q, lo, role, device):
        ref = f_at(d, q, h, lo)
        send(ref, ref, role, device)

    def f_arrive(d, q, lo, tag):
        wait(f_at(d, q, h, lo), f"f{d}{q}{tag}")

    def f_sib(d, q, lo, tag):
        f_send(d, q, lo, f"sf{d}{q}{tag}", sib)

    for lo, tag in parts:
        f_arrive(0, 0, lo, tag)
        f_send(0, 0, lo, "f30" + tag, xp)
        f_send(0, 0, lo, "f10" + tag, xm)
        f_send(0, 0, lo, "f01" + tag, zp)
        f_sib(0, 0, lo, tag)

    def out_unit(d, q, hh):
        k = kap(x + d, zl + q, hh)

        @pl.when(k <= p)
        def _():
            step = rows // 3

            def part(j, carry):
                at = pl.ds(pl.multiple_of(hh * rows + j * step, 64), step)
                o_ref[at, :] += lax.dot_general(
                    fbuf[k, at, :], lbuf[k], (((1,), (1,)), ((), ())),
                    preferred_element_type=F32)
                return carry

            lax.fori_loop(0, 3, part, 0)

    def out_stage(blocks):
        for d, q in blocks:
            for lo, tag in parts:
                wait(f_at(d, q, 1 - h, lo), f"sf{d}{q}{tag}")
        first = blocks[0]

        def step(i, carry):
            j, hh = i // 2, i % 2
            d, q = first
            for n, (dd, qq) in enumerate(blocks[1:], 1):
                d = jnp.where(j == n, dd, d)
                q = jnp.where(j == n, qq, q)
            out_unit(d, q, hh)
            return carry

        lax.fori_loop(0, 2 * len(blocks), step, 0)

    out_stage([(0, 0)])
    (top, _), (bot, _) = parts
    f_arrive(3, 0, top, "t")
    f_send(3, 0, top, "f20t", xp)
    f_sib(3, 0, top, "t")
    f_arrive(1, 0, top, "t")
    f_sib(1, 0, top, "t")
    f_arrive(0, 1, top, "t")
    f_send(0, 1, top, "f31t", xp)
    f_send(0, 1, top, "f11t", xm)
    f_sib(0, 1, top, "t")
    f_arrive(1, 0, bot, "b")
    f_send(1, 0, bot, "f20b", xm)
    f_sib(1, 0, bot, "b")
    f_arrive(3, 0, bot, "b")
    f_sib(3, 0, bot, "b")
    f_arrive(0, 1, bot, "b")
    f_send(0, 1, bot, "f31b", xp)
    f_send(0, 1, bot, "f11b", xm)
    f_sib(0, 1, bot, "b")
    out_stage([(3, 0), (1, 0), (0, 1)])
    for lo, tag in parts:
        f_arrive(2, 0, lo, tag)
        f_send(2, 0, lo, "f21" + tag, zp)
        f_sib(2, 0, lo, tag)
    out_stage([(2, 0)])
    for lo, tag in parts:
        for d in (3, 1):
            f_arrive(d, 1, lo, tag)
            f_sib(d, 1, lo, tag)
    out_stage([(3, 1), (1, 1)])
    for lo, tag in parts:
        f_arrive(2, 1, lo, tag)
        f_sib(2, 1, lo, tag)
    out_stage([(2, 1)])

    for cp in sends:
        cp.wait_send()

    @pl.when(jnp.logical_not(t_self))
    def _():
        for cp in turn:
            cp.wait_send()


SENDS, RECVS = 96, 96


def body(matrix, inverse_factor):
    rows, cols = matrix.shape
    order = 16 * rows
    return pl.pallas_call(
        kernel,
        out_shape=jax.ShapeDtypeStruct((cols, rows), F32),
        in_specs=[pl.BlockSpec(memory_space=pl.ANY)] * 2,
        out_specs=pl.BlockSpec(memory_space=pltpu.VMEM),
        scratch_shapes=[
            pltpu.VMEM((order, cols), BF16),
            pltpu.VMEM((8, rows, cols), BF16),
            pltpu.VMEM((8, cols, cols), BF16),
            pltpu.VMEM((rows, cols), F32),
            pltpu.VMEM((rows, cols), BF16),
            pltpu.SemaphoreType.DMA((SENDS,)),
            pltpu.SemaphoreType.DMA((RECVS,)),
            pltpu.SemaphoreType.DMA((2,)),
        ],
        compiler_params=pltpu.CompilerParams(
            collective_id=0, has_side_effects=True, vmem_limit_bytes=63 * 1024 * 1024),
        cost_estimate=pl.CostEstimate(
            flops=4 * rows * cols * order, bytes_accessed=8 * rows * cols, transcendentals=0),
    )(matrix, inverse_factor)


def solution(mesh):
    in_specs = (P("row", "col"), P("row", "col"))
    return jax.shard_map(body, mesh=mesh, in_specs=in_specs, out_specs=P("col", "row"), check_vma=False)
```

time: 646 us -> 242 us (0.37)
  waiting for transfers between devices: 587 us -> 0 us
  Pallas kernels: 0 us -> 238 us
  matrix products: 41.5 us -> 0 us
  between operations: 13.1 us -> 0.01 us
    all_gather x3 -> x0, waiting for transfers between devices: 357 us -> none  [the longest x1 129 us: body(): lower_rows = lax.all_gather(inverse_factor, 'col', axis=1, tiled=True)]
    pallas_call x0 -> x1, Pallas kernels: none -> 238 us  [body(): pl.pallas_call(kernel, out_shape=jax.ShapeDtypeStruct((cols, rows), F32),...]
    reduce_scatter x1 -> x0, waiting for transfers between devices: 228 us -> none  [body(): lax.psum_scatter(lax.dot_general(column_panel, inverse_factor, contract,...]
    dot_general x2 -> x0, matrix products: 41.5 us -> none  [the longest x1 22.1 us: body(): lax.dot_general(column_panel, inverse_factor, contract, preferred_element...]
  transfers between devices with their start and end apart: 4 -> 0, of which waited for: 4 -> 0; matrix products, arithmetic and copies ran while one was open for 0% -> 0% of each run, Pallas kernels for 0% -> 0%
where the time goes in v1:
time: 242 us; the launch traced here: 241 us
  Pallas kernels  238 us (98%)
  local copies, waits for them, and re-layouts  3.43 us (1%)
    pallas_call x1, Pallas kernels, body(): pl.pallas_call(kernel, out_shape=jax.ShapeDtypeStruct((cols, rows), F32),...  238 us

profile of v1, /device:TPU:63, one launch (start us, length us, event | category | flops | bytes accessed | tf_op | source)
XLA Modules:
  0.0 241.4 jit_solution(17324679166780818790)
XLA Ops:
  0.0 237.9 %shard_map.28 = f32[1152,576]{1,0:T(8,128)} custom-call(bf16[576,1152]{1,0:T(8,128)(2,1)} %a_ref.1, bf16[576,1152]{1,0:T(8,128)(2,1)} %l_ref.1), custom_call_target="tpu_custom_call" | custom-call | flops 24461180928 | bytes 5308416 | tf_op jit(solution)/shard_map/pallas_call | solution.py:305
  238.0 3.4 %copy.3 = f32[1152,576]{0,1:T(8,128)} copy(f32[1152,576]{1,0:T(8,128)} %shard_map.28) | data formatting | bytes 5308416 | tf_op jit(solution)/shard_map/pallas_call | solution.py:305

commit v2 on v0

v2 whole, which is shorter than its diff:
```python
import jax
import jax.numpy as jnp
from jax import lax
from jax.experimental import pallas as pl
from jax.experimental.pallas import tpu as pltpu
from jax.sharding import PartitionSpec as P

BF16, F32 = jnp.bfloat16, jnp.float32


def kernel(a_ref, l_ref, o_ref, abuf, lbuf, fbuf, acc, lbf, ssem, rsem, csem):
    rows, cols = a_ref.shape
    row, c = lax.axis_index("row"), lax.axis_index("col")
    h, p = row % 2, row // 2
    x, zl = p % 4, p // 4
    y, zh = c // 2, c % 2

    def chip(px, pz):
        return (pz % 2) * 4 + px % 4

    def on_row(pp):
        return (pp * 2 + h, c)

    xp, xm = on_row(chip(x + 1, zl)), on_row(chip(x + 3, zl))
    zp = on_row(chip(x, zl + 1))
    sib = (p * 2 + 1 - h, c)
    yp = (row, ((y + 1) % 4) * 2 + zh)
    ym = (row, ((y + 3) % 4) * 2 + zh)
    hp = (row, y * 2 + 1 - zh)

    t_chip = chip(x + y + 2 * h, zh)
    t_dst = (t_chip * 2 + h, p)

    def kap(px, pz, hh):
        return 2 * ((px - c % 4 - 2 * hh + 8) % 4) + pz % 2

    t_src = (c * 2 + h, kap(x, zl, h))
    t_self = (p == c) & (t_chip == p)

    half = rows // 2
    quarter = half // 2
    send_n = [0]
    recv_ids = {}
    sends = []

    def when(cond, f):
        if cond is None:
            f()
        else:
            pl.when(cond)(f)

    def rid(role):
        return recv_ids.setdefault(role, len(recv_ids))

    def send(src, dst, role, device, cond=None):
        i = send_n[0]
        send_n[0] += 1
        cp = pltpu.make_async_remote_copy(
            src, dst, ssem.at[i], rsem.at[rid(role)], device_id=device,
            device_id_type=pl.DeviceIdType.MESH)
        when(cond, cp.start)
        sends.append((cond, cp))

    def drain():
        for cond, cp in sends:
            when(cond, cp.wait_send)
        sends.clear()

    def wait(ref, role, cond=None):
        cp = pltpu.make_async_remote_copy(
            ref, ref, ssem.at[0], rsem.at[rid(role)], device_id=xp,
            device_id_type=pl.DeviceIdType.MESH)
        when(cond, cp.wait_recv)

    barrier = pltpu.get_barrier_semaphore()
    for device in (xp, xm, zp, sib, yp, ym, hp):
        pl.semaphore_signal(barrier, inc=1, device_id=device, device_id_type=pl.DeviceIdType.MESH)

    @pl.when(jnp.logical_not(t_self))
    def _():
        for device in (t_dst, t_src):
            pl.semaphore_signal(barrier, inc=1, device_id=device, device_id_type=pl.DeviceIdType.MESH)

    pl.semaphore_wait(barrier, jnp.where(t_self, 7, 9))

    pieces = {"": (0, rows), "t": (0, half), "b": (half, half),
              "t0": (0, quarter), "t1": (quarter, quarter),
              "b0": (half, quarter), "b1": (half + quarter, quarter)}
    upper, lower = zl == 1, zl == 0

    def need(d):
        return upper | ((y + d) % 4 <= 1)

    def a_at(d, q, hh, piece):
        lo, n = pieces[piece]
        start = pl.multiple_of((chip(x + d, zl + q) * 2 + hh) * rows + lo, 16)
        return abuf.at[pl.ds(start, n)]

    def l_at(d, q, piece):
        lo, n = pieces[piece]
        return lbuf.at[((y + d) % 4) * 2 + (zh + q) % 2, pl.ds(lo, n)]

    def own(ref, piece):
        lo, n = pieces[piece]
        return ref.at[pl.ds(lo, n)]

    def cond_a(q):
        return upper if q else None

    def a_get(d, q, piece):
        ref = a_at(d, q, h, piece)
        wait(ref, f"a{d}{q}{piece}", cond_a(q))
        send(ref, ref, f"sa{d}{q}{piece}", sib, cond_a(q))

    def a_fwd(d, q, piece, to, device, cond):
        ref = a_at(d, q, h, piece)
        send(ref, ref, f"a{to}{piece}", device, cond)

    def a_sib(d, q, *names):
        for piece in names:
            wait(a_at(d, q, 1 - h, piece), f"sa{d}{q}{piece}", cond_a(q))

    def l_get(d, q, piece):
        wait(l_at(d, q, piece), f"l{d}{q}{piece}", need(d))

    def l_fwd(d, q, piece, to, device):
        ref = l_at(d, q, piece)
        send(ref, ref, f"l{to}{piece}", device, need(d))

    tile = 384

    def left_stage(stage, piece):
        lo, n = pieces[piece]
        at_rows = pl.ds(lo, n)
        l_far = (3, 4) if piece == "t" else (5, 5)

        def stage_of(d, q, odd, opposite):
            near = jnp.where(d == 2, 2, 1)
            far = jnp.where(d == 0, 3, jnp.where(d == 2, opposite, odd))
            return jnp.maximum(jnp.where(q == 0, near, far), 2)

        def step(k, carry):
            sa = stage_of((k % 4 - x + 4) % 4, (k // 4 + zl) % 2, 4, 5)
            sl = stage_of((k // 2 - y + 4) % 4, (k % 2 + zh) % 2, *l_far)

            @pl.when((jnp.maximum(sa, sl) == stage) & (k <= p))
            def _():
                krow = pl.multiple_of(k * cols, cols)

                def part(j, carry):
                    at = pl.ds(pl.multiple_of(j * tile, tile), tile)
                    acc[at_rows, at] += jnp.dot(
                        lbuf[k, at_rows], abuf[pl.ds(krow, cols), at],
                        preferred_element_type=F32)
                    return carry

                lax.fori_loop(0, cols // tile, part, 0)
            return carry

        lax.fori_loop(0, 8, step, 0)

    for piece in "tb":
        a_own, l_own = own(a_ref, piece), own(l_ref, piece)
        send(a_own, a_at(0, 0, h, piece), "a30" + piece, xp)
        send(l_own, l_at(0, 0, piece), "l30" + piece, yp, need(0))
        send(a_own, a_at(0, 0, h, piece), "a10" + piece, xm)
        send(l_own, l_at(0, 0, piece), "l10" + piece, ym, need(0))
        if piece == "t":
            first = len(sends)
            send(a_own, a_at(0, 0, h, piece), "a01" + piece, zp, lower)
            send(l_own, l_at(0, 0, piece), "l01" + piece, hp, need(0))
    send(a_ref, a_at(0, 0, h, ""), "sa00", sib)
    ca = pltpu.make_async_copy(a_ref, a_at(0, 0, h, ""), csem.at[0])
    cl = pltpu.make_async_copy(l_ref, l_at(0, 0, ""), csem.at[1])
    ca.start()
    cl.start()
    acc[...] = jnp.zeros_like(acc)
    o_ref[...] = jnp.zeros_like(o_ref)
    ca.wait()
    cl.wait()

    l_get(3, 0, "t")
    l_fwd(3, 0, "t0", "20", yp)
    l_get(1, 0, "t")
    l_fwd(1, 0, "t1", "20", ym)
    a_get(3, 0, "t")
    a_fwd(3, 0, "t", "20", xp, None)
    a_get(1, 0, "t")
    for cond, cp in sends[first:first + 2]:
        when(cond, cp.wait_send)
    del sends[first:first + 2]
    send(own(a_ref, "b"), a_at(0, 0, h, "b"), "a01b", zp, lower)
    send(own(l_ref, "b"), l_at(0, 0, "b"), "l01b", hp, need(0))
    a_get(3, 0, "b")
    a_get(1, 0, "b")
    a_fwd(1, 0, "b", "20", xm, None)
    l_get(0, 1, "t")
    l_fwd(0, 1, "t", "31", yp)
    l_fwd(0, 1, "t", "11", ym)
    a_get(0, 1, "t")
    a_fwd(0, 1, "t", "31", xp, upper)
    a_fwd(0, 1, "t", "11", xm, upper)
    l_get(3, 0, "b")
    l_fwd(3, 0, "b0", "20", yp)
    l_get(1, 0, "b")
    l_fwd(1, 0, "b1", "20", ym)

    a_get(2, 0, "t")
    a_fwd(2, 0, "t", "21", zp, lower)
    a_get(2, 0, "b")
    for piece in ("t0", "t1", "b0", "b1"):
        l_get(2, 0, piece)
    a_sib(0, 0, "")
    a_sib(3, 0, "t", "b")
    a_sib(1, 0, "t", "b")
    a_sib(2, 0, "t", "b")
    left_stage(2, "t")
    left_stage(2, "b")

    l_get(0, 1, "b")
    l_fwd(0, 1, "b", "31", yp)
    l_fwd(0, 1, "b", "11", ym)
    a_get(0, 1, "b")
    a_fwd(0, 1, "b", "31", xp, upper)
    a_fwd(0, 1, "b", "11", xm, upper)
    l_get(3, 1, "t")
    l_fwd(3, 1, "t0", "21", yp)
    l_get(1, 1, "t")
    l_fwd(1, 1, "t1", "21", ym)
    a_sib(0, 1, "t", "b")
    left_stage(3, "t")
    left_stage(3, "b")

    a_get(3, 1, "t")
    a_get(1, 1, "t")
    a_get(3, 1, "b")
    a_fwd(3, 1, "b0", "21", xp, upper)
    a_get(1, 1, "b")
    a_fwd(1, 1, "b1", "21", xm, upper)
    l_get(2, 1, "t0")
    l_get(2, 1, "t1")
    a_sib(3, 1, "t", "b")
    a_sib(1, 1, "t", "b")
    left_stage(4, "t")
    left_stage(4, "b")
    l_get(3, 1, "b")
    l_fwd(3, 1, "b0", "21", yp)
    l_get(1, 1, "b")
    l_fwd(1, 1, "b1", "21", ym)
    a_get(2, 1, "t")
    a_get(2, 1, "b0")
    a_get(2, 1, "b1")
    a_sib(2, 1, "t", "b0", "b1")

    def f_at(d, q, hh, piece):
        lo, n = pieces[piece]
        start = pl.multiple_of(hh * rows + lo, 16)
        return fbuf.at[kap(x + d, zl + q, hh), pl.ds(start, n)]

    turn = []

    def finish(piece):
        left_stage(5, piece)
        lo, n = pieces[piece]
        lbf[pl.ds(lo, n)] = acc[pl.ds(lo, n)].astype(BF16)
        src = lbf.at[pl.ds(lo, n)]
        dst = fbuf.at[c, pl.ds(pl.multiple_of(h * rows + lo, 16), n)]
        i = send_n[0]
        send_n[0] += 1
        landed = rsem.at[rid("f00" + piece)]
        cp = pltpu.make_async_remote_copy(
            src, dst, ssem.at[i], landed, device_id=t_dst,
            device_id_type=pl.DeviceIdType.MESH)
        when(jnp.logical_not(t_self), cp.start)
        when(t_self, lambda: pltpu.make_async_copy(src, dst, landed).start())
        sends.append((jnp.logical_not(t_self), cp))

    finish("t")
    l_get(2, 1, "b0")
    l_get(2, 1, "b1")
    finish("b")

    def f_get(d, q, piece):
        ref = f_at(d, q, h, piece)
        wait(ref, f"f{d}{q}{piece}")
        send(ref, ref, f"sf{d}{q}{piece}", sib)

    def f_fwd(d, q, piece, to, device):
        ref = f_at(d, q, h, piece)
        send(ref, ref, f"f{to}{piece}", device)

    def out_stage(blocks):
        for d, q, piece in blocks:
            wait(f_at(d, q, 1 - h, piece), f"sf{d}{q}{piece}")

        def pick(j, values):
            v = values[0]
            for n, value in enumerate(values[1:], 1):
                v = jnp.where(j == n, value, v)
            return v

        def step(i, carry):
            j, hh = i // 2, i % 2
            d, q = pick(j, [b[0] for b in blocks]), pick(j, [b[1] for b in blocks])
            lo = pick(j, [pieces[b[2]][0] for b in blocks])
            k = kap(x + d, zl + q, hh)

            @pl.when(k <= p)
            def _():
                at = pl.ds(pl.multiple_of(hh * rows + lo, half), half)
                o_ref[at, :] += lax.dot_general(
                    fbuf[k, at, :], lbuf[k], (((1,), (1,)), ((), ())),
                    preferred_element_type=F32)
            return carry

        lax.fori_loop(0, 2 * len(blocks), step, 0)

    for piece in "tb":
        f_get(0, 0, piece)
        f_fwd(0, 0, piece, "30", xp)
        f_fwd(0, 0, piece, "10", xm)
        f_fwd(0, 0, piece, "01", zp)
    f_get(3, 0, "t")
    f_fwd(3, 0, "t", "20", xp)
    f_get(1, 0, "t")
    f_get(0, 1, "t")
    f_fwd(0, 1, "t", "31", xp)
    f_fwd(0, 1, "t", "11", xm)
    f_get(1, 0, "b")
    f_fwd(1, 0, "b", "20", xm)
    f_get(3, 0, "b")
    f_get(0, 1, "b")
    f_fwd(0, 1, "b", "31", xp)
    f_fwd(0, 1, "b", "11", xm)
    out_stage([(0, 0, "t"), (0, 0, "b")])
    f_get(2, 0, "t")
    f_fwd(2, 0, "t", "21", zp)
    f_get(2, 0, "b")
    f_fwd(2, 0, "b", "21", zp)
    out_stage([(3, 0, "t"), (1, 0, "t"), (0, 1, "t"), (3, 0, "b"), (1, 0, "b"), (0, 1, "b")])
    out_stage([(2, 0, "t"), (2, 0, "b")])
    f_get(3, 1, "t")
    f_get(1, 1, "t")
    f_get(2, 1, "t")
    out_stage([(3, 1, "t"), (1, 1, "t"), (2, 1, "t")])
    f_get(2, 1, "b")
    f_get(3, 1, "b")
    f_get(1, 1, "b")
    out_stage([(2, 1, "b"), (3, 1, "b"), (1, 1, "b")])
    drain()


SENDS, RECVS = 160, 160


def body(matrix, inverse_factor):
    rows, cols = matrix.shape
    order = 16 * rows
    return pl.pallas_call(
        kernel,
        out_shape=jax.ShapeDtypeStruct((cols, rows), F32),
        in_specs=[pl.BlockSpec(memory_space=pl.ANY)] * 2,
        out_specs=pl.BlockSpec(memory_space=pltpu.VMEM),
        scratch_shapes=[
            pltpu.VMEM((order, cols), BF16),
            pltpu.VMEM((8, rows, cols), BF16),
            pltpu.VMEM((8, cols, cols), BF16),
            pltpu.VMEM((rows, cols), F32),
            pltpu.VMEM((rows, cols), BF16),
            pltpu.SemaphoreType.DMA((SENDS,)),
            pltpu.SemaphoreType.DMA((RECVS,)),
            pltpu.SemaphoreType.DMA((2,)),
        ],
        compiler_params=pltpu.CompilerParams(
            collective_id=0, has_side_effects=True, vmem_limit_bytes=63 * 1024 * 1024),
        cost_estimate=pl.CostEstimate(
            flops=4 * rows * cols * order, bytes_accessed=8 * rows * cols, transcendentals=0),
    )(matrix, inverse_factor)


def solution(mesh):
    in_specs = (P("row", "col"), P("row", "col"))
    return jax.shard_map(body, mesh=mesh, in_specs=in_specs, out_specs=P("col", "row"), check_vma=False)
```

time: 646 us -> 248 us (0.38)
  the two profiles are of different devices: /device:TPU:63 before, /device:TPU:52 now
where the time goes in v2:
time: 248 us
  Pallas kernels  245 us (99%)
  local copies, waits for them, and re-layouts  3.43 us (1%)
    pallas_call x1, Pallas kernels, body(): pl.pallas_call(kernel, out_shape=jax.ShapeDtypeStruct((cols, rows), F32),...  245 us

profile of v2, /device:TPU:52, one launch (start us, length us, event | category | flops | bytes accessed | tf_op | source)
XLA Modules:
  0.0 248.1 jit_solution(8805585734891862021)
XLA Ops:
  0.0 244.7 %shard_map.28 = f32[1152,576]{1,0:T(8,128)} custom-call(bf16[576,1152]{1,0:T(8,128)(2,1)} %a_ref.1, bf16[576,1152]{1,0:T(8,128)(2,1)} %l_ref.1), custom_call_target="tpu_custom_call" | custom-call | flops 24461180928 | bytes 5308416 | tf_op jit(solution)/shard_map/pallas_call | solution.py:359
  244.7 3.4 %copy.3 = f32[1152,576]{0,1:T(8,128)} copy(f32[1152,576]{1,0:T(8,128)} %shard_map.28) | data formatting | bytes 5308416 | tf_op jit(solution)/shard_map/pallas_call | solution.py:359

commit v3 on v0

v3 whole, which is shorter than its diff:
```python
import jax
import jax.numpy as jnp
from jax import lax
from jax.experimental import pallas as pl
from jax.experimental.pallas import tpu as pltpu
from jax.sharding import PartitionSpec as P

BF16, F32 = jnp.bfloat16, jnp.float32


def kernel(a_ref, l_ref, o_ref, abuf, lbuf, fbuf, acc, lbf, ssem, rsem, csem):
    rows, cols = a_ref.shape
    row, c = lax.axis_index("row"), lax.axis_index("col")
    h, p = row % 2, row // 2
    x, zl = p % 4, p // 4
    y, zh = c // 2, c % 2

    def chip(px, pz):
        return (pz % 2) * 4 + px % 4

    def on_row(pp):
        return (pp * 2 + h, c)

    xp, xm = on_row(chip(x + 1, zl)), on_row(chip(x + 3, zl))
    zp = on_row(chip(x, zl + 1))
    sib = (p * 2 + 1 - h, c)
    yp = (row, ((y + 1) % 4) * 2 + zh)
    ym = (row, ((y + 3) % 4) * 2 + zh)
    hp = (row, y * 2 + 1 - zh)

    t_chip = chip(x + y + 2 * h, zh)
    t_dst = (t_chip * 2 + h, p)

    def kap(px, pz, hh):
        return 2 * ((px - c % 4 - 2 * hh + 8) % 4) + pz % 2

    t_src = (c * 2 + h, kap(x, zl, h))
    t_self = (p == c) & (t_chip == p)

    half = rows // 2
    send_n = [0]
    recv_ids = {}
    sends = []

    def when(cond, f):
        if cond is None:
            f()
        else:
            pl.when(cond)(f)

    def rid(role):
        return recv_ids.setdefault(role, len(recv_ids))

    def send(src, dst, role, device, cond=None):
        i = send_n[0]
        send_n[0] += 1
        cp = pltpu.make_async_remote_copy(
            src, dst, ssem.at[i], rsem.at[rid(role)], device_id=device,
            device_id_type=pl.DeviceIdType.MESH)
        when(cond, cp.start)
        sends.append((cond, cp))

    def drain():
        for cond, cp in sends:
            when(cond, cp.wait_send)
        sends.clear()

    def wait(ref, role, cond=None):
        cp = pltpu.make_async_remote_copy(
            ref, ref, ssem.at[0], rsem.at[rid(role)], device_id=xp,
            device_id_type=pl.DeviceIdType.MESH)
        when(cond, cp.wait_recv)

    barrier = pltpu.get_barrier_semaphore()
    for device in (xp, xm, zp, sib, yp, ym, hp):
        pl.semaphore_signal(barrier, inc=1, device_id=device, device_id_type=pl.DeviceIdType.MESH)

    @pl.when(jnp.logical_not(t_self))
    def _():
        for device in (t_dst, t_src):
            pl.semaphore_signal(barrier, inc=1, device_id=device, device_id_type=pl.DeviceIdType.MESH)

    pl.semaphore_wait(barrier, jnp.where(t_self, 7, 9))

    quarter = half // 2
    row_part = {"": (0, rows), "t": (0, half), "b": (half, half),
                "t0": (0, quarter), "t1": (quarter, quarter),
                "b0": (half, quarter), "b1": (half + quarter, quarter)}
    split = (cols // 256 + 1) * 128
    col_part = {"": (0, cols), "L": (0, split), "R": (split, cols - split)}
    upper, lower = zl == 1, zl == 0

    def cut(ref, start, rp, cp):
        lo, n = row_part[rp]
        at, m = col_part[cp]
        return ref.at[pl.ds(pl.multiple_of(start + lo, 16), n), pl.ds(at, m)]

    def need(d):
        return upper | ((y + d) % 4 <= 1)

    def a_at(d, q, hh, rp, cp):
        return cut(abuf, (chip(x + d, zl + q) * 2 + hh) * rows, rp, cp)

    def l_at(d, q, rp):
        return cut(lbuf.at[((y + d) % 4) * 2 + (zh + q) % 2], 0, rp, "")

    def cond_a(q):
        return upper if q else None

    def a_get(d, q, rp, cp):
        ref = a_at(d, q, h, rp, cp)
        wait(ref, f"a{d}{q}{rp}{cp}", cond_a(q))
        send(ref, ref, f"sa{d}{q}{rp}{cp}", sib, cond_a(q))

    def a_fwd(d, q, rp, cp, to, device, cond):
        ref = a_at(d, q, h, rp, cp)
        send(ref, ref, f"a{to}{rp}{cp}", device, cond)

    def a_sib(d, q, cp, *names):
        for rp in names:
            wait(a_at(d, q, 1 - h, rp, cp), f"sa{d}{q}{rp}{cp}", cond_a(q))

    def l_get(d, q, rp):
        wait(l_at(d, q, rp), f"l{d}{q}{rp}", need(d))

    def l_fwd(d, q, rp, to, device):
        ref = l_at(d, q, rp)
        send(ref, ref, f"l{to}{rp}", device, need(d))

    def a_own(cp, ways):
        src = cut(a_ref, 0, "", cp)
        for role, device, cond in ways:
            send(src, a_at(0, 0, h, "", cp), f"a{role}{cp}", device, cond)

    def l_own(rp, ways):
        src = cut(l_ref, 0, rp, "")
        for role, device in ways:
            send(src, l_at(0, 0, rp), f"l{role}{rp}", device, need(0))

    def left_stage(stage, rp, cp):
        lo, n = row_part[rp]
        at, m = col_part[cp]
        at_rows, at_cols = pl.ds(lo, n), pl.ds(at, m)

        def stage_of(d, q, first):
            return jnp.where((q == 0) | (d == 0), first, first + 1)

        def step(k, carry):
            sa = stage_of((k % 4 - x + 4) % 4, (k // 4 + zl) % 2, 1 if cp == "L" else 3)
            sl = stage_of((k // 2 - y + 4) % 4, (k % 2 + zh) % 2, 1 if rp == "t" else 3)

            @pl.when((jnp.maximum(sa, sl) == stage) & (k <= p))
            def _():
                krow = pl.multiple_of(k * cols, cols)
                acc[at_rows, at_cols] += jnp.dot(
                    lbuf[k, at_rows], abuf[pl.ds(krow, cols), at_cols],
                    preferred_element_type=F32)

            return carry

        lax.fori_loop(0, 8, step, 0)

    def f_at(d, q, hh, rp, cp):
        return cut(fbuf.at[kap(x + d, zl + q, hh)], hh * rows, rp, cp)

    def finish(rp, cp):
        lo, n = row_part[rp]
        at, m = col_part[cp]
        lbf[pl.ds(lo, n), pl.ds(at, m)] = acc[pl.ds(lo, n), pl.ds(at, m)].astype(BF16)
        src = cut(lbf, 0, rp, cp)
        dst = cut(fbuf.at[c], h * rows, rp, cp)
        i = send_n[0]
        send_n[0] += 1
        landed = rsem.at[rid(f"f00{rp}{cp}")]
        copy = pltpu.make_async_remote_copy(
            src, dst, ssem.at[i], landed, device_id=t_dst,
            device_id_type=pl.DeviceIdType.MESH)
        when(jnp.logical_not(t_self), copy.start)
        when(t_self, lambda: pltpu.make_async_copy(src, dst, landed).start())
        sends.append((jnp.logical_not(t_self), copy))

    def f_fwd(d, q, piece, to, device):
        ref = f_at(d, q, h, *piece)
        send(ref, ref, "f" + to + piece, device)

    def f_get(piece, *roles):
        for d, q in roles:
            ref = f_at(d, q, h, *piece)
            wait(ref, f"f{d}{q}{piece}")
            if (d, q) == (0, 0):
                f_fwd(d, q, piece, "30", xp)
                f_fwd(d, q, piece, "10", xm)
                f_fwd(d, q, piece, "01", zp)
            elif (d, q) == (3, 0) and piece[0] == "t":
                f_fwd(d, q, piece, "20", xp)
            elif (d, q) == (1, 0) and piece[0] == "b":
                f_fwd(d, q, piece, "20", xm)
            elif (d, q) == (0, 1):
                f_fwd(d, q, piece, "31", xp)
                f_fwd(d, q, piece, "11", xm)
            elif (d, q) == (2, 0):
                f_fwd(d, q, piece, "21", zp)
            send(ref, ref, f"sf{d}{q}{piece}", sib)

    def out_stage(cp, *roles):
        for d, q in roles:
            for rp in "tb":
                wait(f_at(d, q, 1 - h, rp, cp), f"sf{d}{q}{rp}{cp}")
        at_cols = pl.ds(*col_part[cp])

        def pick(j, values):
            v = values[0]
            for n, value in enumerate(values[1:], 1):
                v = jnp.where(j == n, value, v)
            return v

        def step(i, carry):
            j, hh = i // 2, i % 2
            d, q = pick(j, [r[0] for r in roles]), pick(j, [r[1] for r in roles])
            k = kap(x + d, zl + q, hh)

            @pl.when(k <= p)
            def _():
                at = pl.ds(pl.multiple_of(hh * rows, rows), rows)
                o_ref[at, :] += lax.dot_general(
                    fbuf[k, at, at_cols], lbuf[k, :, at_cols], (((1,), (1,)), ((), ())),
                    preferred_element_type=F32)
            return carry

        lax.fori_loop(0, 2 * len(roles), step, 0)

    ring = (("30", xp, None), ("10", xm, None))
    a_own("L", ring)
    l_own("t", (("30", yp), ("10", ym)))
    first = len(sends)
    a_own("L", (("01", zp, lower),))
    l_own("t", (("01", hp),))
    send(a_ref, a_at(0, 0, h, "", ""), "sa00", sib)
    ca = pltpu.make_async_copy(a_ref, a_at(0, 0, h, "", ""), csem.at[0])
    cl = pltpu.make_async_copy(l_ref, l_at(0, 0, ""), csem.at[1])
    ca.start()
    cl.start()
    acc[...] = jnp.zeros_like(acc)
    o_ref[...] = jnp.zeros_like(o_ref)
    ca.wait()
    cl.wait()

    l_get(3, 0, "t")
    l_fwd(3, 0, "t0", "20", yp)
    l_get(1, 0, "t")
    l_fwd(1, 0, "t1", "20", ym)
    l_own("b", (("30", yp), ("10", ym)))
    a_get(3, 0, "", "L")
    a_fwd(3, 0, "t", "L", "20", xp, None)
    a_get(1, 0, "", "L")
    a_fwd(1, 0, "b", "L", "20", xm, None)
    a_own("R", ring)
    for cond, copy in sends[first:first + 2]:
        when(cond, copy.wait_send)
    del sends[first:first + 2]
    a_own("R", (("01", zp, lower),))
    l_own("b", (("01", hp),))
    l_get(0, 1, "t")
    l_fwd(0, 1, "t", "31", yp)
    l_fwd(0, 1, "t", "11", ym)
    a_get(0, 1, "", "L")
    a_fwd(0, 1, "", "L", "31", xp, upper)
    a_fwd(0, 1, "", "L", "11", xm, upper)
    a_get(2, 0, "t", "L")
    a_fwd(2, 0, "t", "L", "21", zp, lower)
    a_get(2, 0, "b", "L")
    l_get(3, 0, "b")
    l_fwd(3, 0, "b0", "20", yp)
    l_get(1, 0, "b")
    l_fwd(1, 0, "b1", "20", ym)
    a_get(3, 0, "", "R")
    a_fwd(3, 0, "t", "R", "20", xp, None)
    a_get(1, 0, "", "R")
    a_fwd(1, 0, "b", "R", "20", xm, None)
    l_get(2, 0, "t0")
    l_get(2, 0, "t1")
    wait(a_at(0, 0, 1 - h, "", ""), "sa00")
    for d in (3, 1):
        a_sib(d, 0, "L", "")
    a_sib(0, 1, "L", "")
    a_sib(2, 0, "L", "t", "b")
    left_stage(1, "t", "L")

    l_get(3, 1, "t")
    l_fwd(3, 1, "t0", "21", yp)
    l_get(1, 1, "t")
    l_fwd(1, 1, "t1", "21", ym)
    a_get(3, 1, "", "L")
    a_fwd(3, 1, "b0", "L", "21", xp, upper)
    a_get(1, 1, "", "L")
    a_fwd(1, 1, "b1", "L", "21", xm, upper)
    l_get(0, 1, "b")
    l_fwd(0, 1, "b", "31", yp)
    l_fwd(0, 1, "b", "11", ym)
    a_get(0, 1, "", "R")
    a_fwd(0, 1, "", "R", "31", xp, upper)
    a_fwd(0, 1, "", "R", "11", xm, upper)
    a_get(2, 0, "t", "R")
    a_fwd(2, 0, "t", "R", "21", zp, lower)
    a_get(2, 0, "b", "R")
    for rp in ("t", "b0", "b1"):
        a_get(2, 1, rp, "L")
    l_get(2, 1, "t0")
    l_get(2, 1, "t1")
    for d in (3, 1):
        a_sib(d, 1, "L", "")
    a_sib(2, 1, "L", "t", "b0", "b1")
    left_stage(2, "t", "L")
    finish("t", "L")

    l_get(2, 0, "b0")
    l_get(2, 0, "b1")
    for d in (3, 1):
        a_sib(d, 0, "R", "")
    a_sib(0, 1, "R", "")
    a_sib(2, 0, "R", "t", "b")
    left_stage(3, "b", "L")
    left_stage(3, "t", "R")
    left_stage(3, "b", "R")

    l_get(3, 1, "b")
    l_fwd(3, 1, "b0", "21", yp)
    l_get(1, 1, "b")
    l_fwd(1, 1, "b1", "21", ym)
    a_get(3, 1, "", "R")
    a_fwd(3, 1, "b0", "R", "21", xp, upper)
    a_get(1, 1, "", "R")
    a_fwd(1, 1, "b1", "R", "21", xm, upper)
    f_get("tL", (0, 0))
    l_get(2, 1, "b0")
    l_get(2, 1, "b1")
    left_stage(4, "b", "L")
    finish("b", "L")
    for rp in ("t", "b0", "b1"):
        a_get(2, 1, rp, "R")
    for d in (3, 1):
        a_sib(d, 1, "R", "")
    a_sib(2, 1, "R", "t", "b0", "b1")
    left_stage(4, "t", "R")
    finish("t", "R")
    f_get("tL", (3, 0), (1, 0), (0, 1))
    left_stage(4, "b", "R")
    finish("b", "R")

    near = ((3, 0), (1, 0), (0, 1))
    far = ((3, 1), (1, 1), (2, 1))
    f_get("tL", (2, 0))
    f_get("bL", (0, 0))
    f_get("tR", (0, 0))
    f_get("bL", *near)
    f_get("bR", (0, 0))
    f_get("tL", *far)
    f_get("tR", *near)
    f_get("bL", (2, 0))
    out_stage("L", (0, 0), *near)
    f_get("bR", *near)
    f_get("tR", (2, 0))
    f_get("bL", *far)
    f_get("bR", (2, 0))
    out_stage("R", (0, 0), *near)
    out_stage("L", (2, 0), *far)
    f_get("tR", *far)
    out_stage("R", (2, 0))
    f_get("bR", *far)
    out_stage("R", *far)
    drain()


SENDS, RECVS = 200, 200


def body(matrix, inverse_factor):
    rows, cols = matrix.shape
    order = 16 * rows
    return pl.pallas_call(
        kernel,
        out_shape=jax.ShapeDtypeStruct((cols, rows), F32),
        in_specs=[pl.BlockSpec(memory_space=pl.ANY)] * 2,
        out_specs=pl.BlockSpec(memory_space=pltpu.VMEM),
        scratch_shapes=[
            pltpu.VMEM((order, cols), BF16),
            pltpu.VMEM((8, rows, cols), BF16),
            pltpu.VMEM((8, cols, cols), BF16),
            pltpu.VMEM((rows, cols), F32),
            pltpu.VMEM((rows, cols), BF16),
            pltpu.SemaphoreType.DMA((SENDS,)),
            pltpu.SemaphoreType.DMA((RECVS,)),
            pltpu.SemaphoreType.DMA((2,)),
        ],
        compiler_params=pltpu.CompilerParams(
            collective_id=0, has_side_effects=True, vmem_limit_bytes=63 * 1024 * 1024),
        cost_estimate=pl.CostEstimate(
            flops=4 * rows * cols * order, bytes_accessed=8 * rows * cols, transcendentals=0),
    )(matrix, inverse_factor)


def solution(mesh):
    in_specs = (P("row", "col"), P("row", "col"))
    return jax.shard_map(body, mesh=mesh, in_specs=in_specs, out_specs=P("col", "row"), check_vma=False)
```

time: 646 us -> 216 us (0.33)
  the two profiles are of different devices: /device:TPU:63 before, /device:TPU:53 now
where the time goes in v3:
time: 216 us
  Pallas kernels  212 us (98%)
  local copies, waits for them, and re-layouts  3.43 us (2%)
    pallas_call x1, Pallas kernels, body(): pl.pallas_call(kernel, out_shape=jax.ShapeDtypeStruct((cols, rows), F32),...  212 us

profile of v3, /device:TPU:53, one launch (start us, length us, event | category | flops | bytes accessed | tf_op | source)
XLA Modules:
  0.0 215.6 jit_solution(6707376136469665668)
XLA Ops:
  0.0 212.2 %shard_map.28 = f32[1152,576]{1,0:T(8,128)} custom-call(bf16[576,1152]{1,0:T(8,128)(2,1)} %a_ref.1, bf16[576,1152]{1,0:T(8,128)(2,1)} %l_ref.1), custom_call_target="tpu_custom_call" | custom-call | flops 24461180928 | bytes 5308416 | tf_op jit(solution)/shard_map/pallas_call | solution.py:380
  212.2 3.4 %copy.3 = f32[1152,576]{0,1:T(8,128)} copy(f32[1152,576]{1,0:T(8,128)} %shard_map.28) | data formatting | bytes 5308416 | tf_op jit(solution)/shard_map/pallas_call | solution.py:380

commit v4 on v3

--- a/solution.py
+++ b/solution.py
@@ -82,11 +82,13 @@
 
     pl.semaphore_wait(barrier, jnp.where(t_self, 7, 9))
 
-    quarter = half // 2
-    row_part = {"": (0, rows), "t": (0, half), "b": (half, half),
-                "t0": (0, quarter), "t1": (quarter, quarter),
-                "b0": (half, quarter), "b1": (half + quarter, quarter)}
-    split = (cols // 256 + 1) * 128
+    top, split = half, (cols // 256 + 1) * 128
+
+    def halves(name, lo, n):
+        return {name: (lo, n), name + "0": (lo, n // 2), name + "1": (lo + n // 2, n // 2)}
+
+    row_part = {"": (0, rows), "u": (0, half), "v": (half, half),
+                **halves("t", 0, top), **halves("b", top, rows - top)}
     col_part = {"": (0, cols), "L": (0, split), "R": (split, cols - split)}
     upper, lower = zl == 1, zl == 0
 
@@ -191,9 +193,9 @@
                 f_fwd(d, q, piece, "30", xp)
                 f_fwd(d, q, piece, "10", xm)
                 f_fwd(d, q, piece, "01", zp)
-            elif (d, q) == (3, 0) and piece[0] == "t":
+            elif (d, q) == (3, 0) and piece in ("tL", "bR"):
                 f_fwd(d, q, piece, "20", xp)
-            elif (d, q) == (1, 0) and piece[0] == "b":
+            elif (d, q) == (1, 0) and piece in ("tR", "bL"):
                 f_fwd(d, q, piece, "20", xm)
             elif (d, q) == (0, 1):
                 f_fwd(d, q, piece, "31", xp)
@@ -202,16 +204,15 @@
                 f_fwd(d, q, piece, "21", zp)
             send(ref, ref, f"sf{d}{q}{piece}", sib)
 
-    def out_stage(cp, *roles):
+    def out_stage(piece, *roles):
         for d, q in roles:
-            for rp in "tb":
-                wait(f_at(d, q, 1 - h, rp, cp), f"sf{d}{q}{rp}{cp}")
-        at_cols = pl.ds(*col_part[cp])
+            wait(f_at(d, q, 1 - h, *piece), f"sf{d}{q}{piece}")
+        (lo, n), at_cols = row_part[piece[0]], pl.ds(*col_part[piece[1]])
 
         def pick(j, values):
             v = values[0]
-            for n, value in enumerate(values[1:], 1):
-                v = jnp.where(j == n, value, v)
+            for i, value in enumerate(values[1:], 1):
+                v = jnp.where(j == i, value, v)
             return v
 
         def step(i, carry):
@@ -221,7 +222,7 @@
 
             @pl.when(k <= p)
             def _():
-                at = pl.ds(pl.multiple_of(hh * rows, rows), rows)
+                at = pl.ds(pl.multiple_of(hh * rows + lo, 32), n)
                 o_ref[at, :] += lax.dot_general(
                     fbuf[k, at, at_cols], lbuf[k, :, at_cols], (((1,), (1,)), ((), ())),
                     preferred_element_type=F32)
@@ -251,9 +252,9 @@
     l_fwd(1, 0, "t1", "20", ym)
     l_own("b", (("30", yp), ("10", ym)))
     a_get(3, 0, "", "L")
-    a_fwd(3, 0, "t", "L", "20", xp, None)
+    a_fwd(3, 0, "u", "L", "20", xp, None)
     a_get(1, 0, "", "L")
-    a_fwd(1, 0, "b", "L", "20", xm, None)
+    a_fwd(1, 0, "v", "L", "20", xm, None)
     a_own("R", ring)
     for cond, copy in sends[first:first + 2]:
         when(cond, copy.wait_send)
@@ -266,24 +267,23 @@
     a_get(0, 1, "", "L")
     a_fwd(0, 1, "", "L", "31", xp, upper)
     a_fwd(0, 1, "", "L", "11", xm, upper)
-    a_get(2, 0, "t", "L")
-    a_fwd(2, 0, "t", "L", "21", zp, lower)
-    a_get(2, 0, "b", "L")
+    a_get(2, 0, "u", "L")
+    a_get(2, 0, "v", "L")
     l_get(3, 0, "b")
     l_fwd(3, 0, "b0", "20", yp)
     l_get(1, 0, "b")
     l_fwd(1, 0, "b1", "20", ym)
     a_get(3, 0, "", "R")
-    a_fwd(3, 0, "t", "R", "20", xp, None)
+    a_fwd(3, 0, "u", "R", "20", xp, None)
     a_get(1, 0, "", "R")
-    a_fwd(1, 0, "b", "R", "20", xm, None)
+    a_fwd(1, 0, "v", "R", "20", xm, None)
     l_get(2, 0, "t0")
     l_get(2, 0, "t1")
     wait(a_at(0, 0, 1 - h, "", ""), "sa00")
     for d in (3, 1):
         a_sib(d, 0, "L", "")
     a_sib(0, 1, "L", "")
-    a_sib(2, 0, "L", "t", "b")
+    a_sib(2, 0, "L", "u", "v")
     left_stage(1, "t", "L")
 
     l_get(3, 1, "t")
@@ -291,25 +291,24 @@
     l_get(1, 1, "t")
     l_fwd(1, 1, "t1", "21", ym)
     a_get(3, 1, "", "L")
-    a_fwd(3, 1, "b0", "L", "21", xp, upper)
+    a_fwd(3, 1, "u", "L", "21", xp, upper)
     a_get(1, 1, "", "L")
-    a_fwd(1, 1, "b1", "L", "21", xm, upper)
+    a_fwd(1, 1, "v", "L", "21", xm, upper)
     l_get(0, 1, "b")
     l_fwd(0, 1, "b", "31", yp)
     l_fwd(0, 1, "b", "11", ym)
     a_get(0, 1, "", "R")
     a_fwd(0, 1, "", "R", "31", xp, upper)
     a_fwd(0, 1, "", "R", "11", xm, upper)
-    a_get(2, 0, "t", "R")
-    a_fwd(2, 0, "t", "R", "21", zp, lower)
-    a_get(2, 0, "b", "R")
-    for rp in ("t", "b0", "b1"):
+    a_get(2, 0, "u", "R")
+    a_get(2, 0, "v", "R")
+    for rp in "uv":
         a_get(2, 1, rp, "L")
     l_get(2, 1, "t0")
     l_get(2, 1, "t1")
     for d in (3, 1):
         a_sib(d, 1, "L", "")
-    a_sib(2, 1, "L", "t", "b0", "b1")
+    a_sib(2, 1, "L", "u", "v")
     left_stage(2, "t", "L")
     finish("t", "L")
 
@@ -318,56 +317,55 @@
     for d in (3, 1):
         a_sib(d, 0, "R", "")
     a_sib(0, 1, "R", "")
-    a_sib(2, 0, "R", "t", "b")
+    a_sib(2, 0, "R", "u", "v")
     left_stage(3, "b", "L")
     left_stage(3, "t", "R")
     left_stage(3, "b", "R")
 
+    a_get(3, 1, "", "R")
+    a_fwd(3, 1, "u", "R", "21", xp, upper)
+    a_get(1, 1, "", "R")
+    a_fwd(1, 1, "v", "R", "21", xm, upper)
     l_get(3, 1, "b")
     l_fwd(3, 1, "b0", "21", yp)
     l_get(1, 1, "b")
     l_fwd(1, 1, "b1", "21", ym)
-    a_get(3, 1, "", "R")
-    a_fwd(3, 1, "b0", "R", "21", xp, upper)
-    a_get(1, 1, "", "R")
-    a_fwd(1, 1, "b1", "R", "21", xm, upper)
     f_get("tL", (0, 0))
+    for rp in "uv":
+        a_get(2, 1, rp, "R")
+    for d in (3, 1):
+        a_sib(d, 1, "R", "")
+    a_sib(2, 1, "R", "u", "v")
+    left_stage(4, "t", "R")
+    finish("t", "R")
     l_get(2, 1, "b0")
     l_get(2, 1, "b1")
     left_stage(4, "b", "L")
     finish("b", "L")
-    for rp in ("t", "b0", "b1"):
-        a_get(2, 1, rp, "R")
-    for d in (3, 1):
-        a_sib(d, 1, "R", "")
-    a_sib(2, 1, "R", "t", "b0", "b1")
-    left_stage(4, "t", "R")
-    finish("t", "R")
-    f_get("tL", (3, 0), (1, 0), (0, 1))
+    near = ((3, 0), (1, 0), (0, 1))
+    far = ((3, 1), (1, 1), (2, 1))
+    f_get("tL", *near)
     left_stage(4, "b", "R")
     finish("b", "R")
 
-    near = ((3, 0), (1, 0), (0, 1))
-    far = ((3, 1), (1, 1), (2, 1))
+    order = (
+        ("tR", 0, 0), ("bL", 0, 0), ("tL", 3, 1), ("tL", 1, 1), ("bR", 0, 0), ("tL", 2, 1),
+        ("tR", 3, 0), ("tR", 1, 0), ("tR", 0, 1), ("bL", 3, 0), ("bL", 1, 0), ("bL", 0, 1),
+        ("bR", 3, 0), ("bR", 1, 0), ("bR", 0, 1), ("tR", 2, 0), ("bL", 2, 0), ("bR", 2, 0),
+        ("tR", 3, 1), ("tR", 1, 1), ("bL", 3, 1), ("bL", 1, 1), ("tR", 2, 1), ("bL", 2, 1),
+        ("bR", 3, 1), ("bR", 1, 1), ("bR", 2, 1),
+    )
+    lag = 3
     f_get("tL", (2, 0))
-    f_get("bL", (0, 0))
-    f_get("tR", (0, 0))
-    f_get("bL", *near)
-    f_get("bR", (0, 0))
-    f_get("tL", *far)
-    f_get("tR", *near)
-    f_get("bL", (2, 0))
-    out_stage("L", (0, 0), *near)
-    f_get("bR", *near)
-    f_get("tR", (2, 0))
-    f_get("bL", *far)
-    f_get("bR", (2, 0))
-    out_stage("R", (0, 0), *near)
-    out_stage("L", (2, 0), *far)
-    f_get("tR", *far)
-    out_stage("R", (2, 0))
-    f_get("bR", *far)
-    out_stage("R", *far)
+    out_stage("tL", (0, 0), *near)
+    out_stage("tL", (2, 0))
+    for i, (piece, *role) in enumerate(order):
+        f_get(piece, tuple(role))
+        if i >= lag:
+            piece, *role = order[i - lag]
+            out_stage(piece, tuple(role))
+    for piece, *role in order[len(order) - lag:]:
+        out_stage(piece, tuple(role))
     drain()
 
 

time: 216 us -> 201 us (0.931)
  the two profiles are of different devices: /device:TPU:53 before, /device:TPU:63 now
where the time goes in v4:
time: 201 us; the launch traced here: 198 us
  Pallas kernels  194 us (97%)
  local copies, waits for them, and re-layouts  3.43 us (2%)
    pallas_call x1, Pallas kernels, body(): pl.pallas_call(kernel, out_shape=jax.ShapeDtypeStruct((cols, rows), F32),...  194 us

profile of v4, /device:TPU:63, one launch (start us, length us, event | category | flops | bytes accessed | tf_op | source)
XLA Modules:
  0.0 197.6 jit_solution(17957802927045583149)
XLA Ops:
  0.0 194.2 %shard_map.28 = f32[1152,576]{1,0:T(8,128)} custom-call(bf16[576,1152]{1,0:T(8,128)(2,1)} %a_ref.1, bf16[576,1152]{1,0:T(8,128)(2,1)} %l_ref.1), custom_call_target="tpu_custom_call" | custom-call | flops 24461180928 | bytes 5308416 | tf_op jit(solution)/shard_map/pallas_call | solution.py:378
  194.2 3.4 %copy.3 = f32[1152,576]{0,1:T(8,128)} copy(f32[1152,576]{1,0:T(8,128)} %shard_map.28) | data formatting | bytes 5308416 | tf_op jit(solution)/shard_map/pallas_call | solution.py:378

commit v5 on v4

--- a/solution.py
+++ b/solution.py
@@ -28,11 +28,11 @@
     ym = (row, ((y + 3) % 4) * 2 + zh)
     hp = (row, y * 2 + 1 - zh)
 
-    t_chip = chip(x + y + 2 * h, zh)
+    t_chip = chip(x + y + 2 * h, zh + h)
     t_dst = (t_chip * 2 + h, p)
 
     def kap(px, pz, hh):
-        return 2 * ((px - c % 4 - 2 * hh + 8) % 4) + pz % 2
+        return 2 * ((px - c % 4 - 2 * hh + 8) % 4) + (pz + hh) % 2
 
     t_src = (c * 2 + h, kap(x, zl, h))
     t_self = (p == c) & (t_chip == p)
@@ -181,14 +181,21 @@
         when(t_self, lambda: pltpu.make_async_copy(src, dst, landed).start())
         sends.append((jnp.logical_not(t_self), copy))
 
+    def f_need(d, q, hh, who):
+        return who | (kap(x + d, zl + q, hh) < 4)
+
     def f_fwd(d, q, piece, to, device):
         ref = f_at(d, q, h, *piece)
-        send(ref, ref, "f" + to + piece, device)
+        cond = None
+        if to[1] == "1":
+            cond = f_need(d, q, h, upper if q else lower)
+        send(ref, ref, "f" + to + piece, device, cond)
 
     def f_get(piece, *roles):
         for d, q in roles:
             ref = f_at(d, q, h, *piece)
-            wait(ref, f"f{d}{q}{piece}")
+            cond = f_need(d, q, h, upper) if q else None
+            wait(ref, f"f{d}{q}{piece}", cond)
             if (d, q) == (0, 0):
                 f_fwd(d, q, piece, "30", xp)
                 f_fwd(d, q, piece, "10", xm)
@@ -202,11 +209,12 @@
                 f_fwd(d, q, piece, "11", xm)
             elif (d, q) == (2, 0):
                 f_fwd(d, q, piece, "21", zp)
-            send(ref, ref, f"sf{d}{q}{piece}", sib)
+            send(ref, ref, f"sf{d}{q}{piece}", sib, cond)
 
     def out_stage(piece, *roles):
         for d, q in roles:
-            wait(f_at(d, q, 1 - h, *piece), f"sf{d}{q}{piece}")
+            cond = f_need(d, q, 1 - h, upper) if q else None
+            wait(f_at(d, q, 1 - h, *piece), f"sf{d}{q}{piece}", cond)
         (lo, n), at_cols = row_part[piece[0]], pl.ds(*col_part[piece[1]])
 
         def pick(j, values):
@@ -231,11 +239,11 @@
         lax.fori_loop(0, 2 * len(roles), step, 0)
 
     ring = (("30", xp, None), ("10", xm, None))
+    first = len(sends)
+    l_own("t", (("01", hp),))
+    a_own("L", (("01", zp, lower),))
     a_own("L", ring)
     l_own("t", (("30", yp), ("10", ym)))
-    first = len(sends)
-    a_own("L", (("01", zp, lower),))
-    l_own("t", (("01", hp),))
     send(a_ref, a_at(0, 0, h, "", ""), "sa00", sib)
     ca = pltpu.make_async_copy(a_ref, a_at(0, 0, h, "", ""), csem.at[0])
     cl = pltpu.make_async_copy(l_ref, l_at(0, 0, ""), csem.at[1])
@@ -355,7 +363,7 @@
         ("tR", 3, 1), ("tR", 1, 1), ("bL", 3, 1), ("bL", 1, 1), ("tR", 2, 1), ("bL", 2, 1),
         ("bR", 3, 1), ("bR", 1, 1), ("bR", 2, 1),
     )
-    lag = 3
+    lag = 2
     f_get("tL", (2, 0))
     out_stage("tL", (0, 0), *near)
     out_stage("tL", (2, 0))

time: 201 us -> 199 us (0.990)
  no operation moved by 1% of the time
where the time goes in v5:
time: 199 us; the launch traced here: 197 us
  Pallas kernels  194 us (97%)
  local copies, waits for them, and re-layouts  3.43 us (2%)
    pallas_call x1, Pallas kernels, body(): pl.pallas_call(kernel, out_shape=jax.ShapeDtypeStruct((cols, rows), F32),...  194 us

profile of v5, /device:TPU:63, one launch (start us, length us, event | category | flops | bytes accessed | tf_op | source)
XLA Modules:
  0.0 197.3 jit_solution(10165436131670522768)
XLA Ops:
  0.0 193.9 %shard_map.28 = f32[1152,576]{1,0:T(8,128)} custom-call(bf16[576,1152]{1,0:T(8,128)(2,1)} %a_ref.1, bf16[576,1152]{1,0:T(8,128)(2,1)} %l_ref.1), custom_call_target="tpu_custom_call" | custom-call | flops 24461180928 | bytes 5308416 | tf_op jit(solution)/shard_map/pallas_call | solution.py:386
  193.9 3.4 %copy.3 = f32[1152,576]{0,1:T(8,128)} copy(f32[1152,576]{1,0:T(8,128)} %shard_map.28) | data formatting | bytes 5308416 | tf_op jit(solution)/shard_map/pallas_call | solution.py:386

commit v6 on v5

--- a/solution.py
+++ b/solution.py
@@ -346,13 +346,14 @@
     a_sib(2, 1, "R", "u", "v")
     left_stage(4, "t", "R")
     finish("t", "R")
+    near = ((3, 0), (1, 0), (0, 1))
+    f_get("tL", *near)
     l_get(2, 1, "b0")
     l_get(2, 1, "b1")
     left_stage(4, "b", "L")
     finish("b", "L")
     near = ((3, 0), (1, 0), (0, 1))
     far = ((3, 1), (1, 1), (2, 1))
-    f_get("tL", *near)
     left_stage(4, "b", "R")
     finish("b", "R")
 

time: 199 us -> 198 us (level)
  no operation moved by 1% of the time
where the time goes in v6:
time: 198 us; the launch traced here: 196 us
  Pallas kernels  193 us (97%)
  local copies, waits for them, and re-layouts  3.43 us (2%)
    pallas_call x1, Pallas kernels, body(): pl.pallas_call(kernel, out_shape=jax.ShapeDtypeStruct((cols, rows), F32),...  193 us

profile of v6, /device:TPU:63, one launch (start us, length us, event | category | flops | bytes accessed | tf_op | source)
XLA Modules:
  0.0 196.3 jit_solution(10713595702896122214)
XLA Ops:
  0.0 192.8 %shard_map.28 = f32[1152,576]{1,0:T(8,128)} custom-call(bf16[576,1152]{1,0:T(8,128)(2,1)} %a_ref.1, bf16[576,1152]{1,0:T(8,128)(2,1)} %l_ref.1), custom_call_target="tpu_custom_call" | custom-call | flops 24461180928 | bytes 5308416 | tf_op jit(solution)/shard_map/pallas_call | solution.py:387
  192.9 3.4 %copy.3 = f32[1152,576]{0,1:T(8,128)} copy(f32[1152,576]{1,0:T(8,128)} %shard_map.28) | data formatting | bytes 5308416 | tf_op jit(solution)/shard_map/pallas_call | solution.py:387
